TPU v7x, 32 devices: a whole 2x2x4 slice. The times are simulated.
32 devices in a mesh: seq: 4 (over y, x), fsdp: 8 (over z, core).
Axes of the slice: x: 2, y: 2, z: 4, core: 2. Of those that a mesh axis runs over, the one named last changes fastest.
Arguments:
- byte_rows: bfloat16 [8, 4096, 512], P('fsdp', 'seq'), may hold values from -6 to 6
- cotangent: bfloat16 [8, 4096, 512], P('fsdp', 'seq'), may hold values from -6 to 6
- doc_ids: int32 [8, 4096], P('fsdp', 'seq'), may hold values from 0 to 7, never falling along the last dimension, each value on 1 to 2048 neighbouring positions
- conv_weight: bfloat16 [8, 32, 16, 16], replicated, may hold values from -0.5 to 0.5
- norm_gain: float32 [512], replicated, may hold values from 0.5 to 1.5
- proj_weight: bfloat16 [4096, 512], P('fsdp'), may hold values from -0.25 to 0.25
- round_seed: int32 [1], replicated, may hold values from 0 to 1073741823
- step_count: int32 [1], replicated, may hold values from 0 to 999999
Outputs:
- grad_bytes: float32 [8, 4096, 512], P('fsdp', 'seq')
- grad_proj: float32 [4096, 512], P('fsdp')
- grad_conv: float32 [8, 32, 16, 16], replicated
- grad_gain: float32 [512], replicated
Inputs may be any that keep to these rules, and one draw needn't show every extreme that they name: `doc_ids`: along each sequence the document numbers never fall; no document covers more than 2048 bytes, and one covers exactly 2048.
All inputs are finite; a program needn't handle non-finite values.
Results may differ from a plain program's by a relative error of at most 0.0046.
Values may be sent and summed in bfloat16 or wider, within the bound.
A program may use at most 128 MiB of HBM per device.

v0:
```python
import math

import jax
import jax.numpy as jnp
from jax import lax
from jax.sharding import PartitionSpec as P

GROUPS = 32
KERNEL = 8
STRIDE = 4
CG = 16


GELU_A = 0.7978845608028654
GELU_B = 0.044715
QUANT = 0.25


def shifted(value, axis, steps):
    count = lax.axis_size(axis)
    initial, last = (max(0, -steps), min(count, count - steps))
    return lax.ppermute(value, axis, [(source, source + steps) for source in range(initial, last)])


def gelu_grad(values):
    tangent = jnp.tanh(GELU_A * (values + GELU_B * values * values * values))
    return 0.5 * (1.0 + tangent) + 0.5 * values * (1.0 - tangent * tangent) * GELU_A * (
        1.0 + 3.0 * GELU_B * values * values
    )


def mix_bits(flat_index, seed_value, step_value):
    hashed = (
        flat_index * jnp.int32(-1640531535)
        + seed_value * jnp.int32(-2048144777)
        + step_value * jnp.int32(-1028477379)
    )
    hashed = hashed ^ lax.shift_right_logical(hashed, jnp.int32(16))
    hashed = hashed * jnp.int32(2146121005)
    hashed = hashed ^ lax.shift_right_logical(hashed, jnp.int32(15))
    hashed = hashed * jnp.int32(-2073254261)
    hashed = hashed ^ lax.shift_right_logical(hashed, jnp.int32(16))
    return lax.shift_right_logical(hashed, jnp.int32(8)).astype(jnp.float32) / 16777216.0


def tap_windows(series, extra_rows, patches):
    joined = jnp.concatenate([series, extra_rows], 0)
    tail_shape = joined.shape[1:]
    lower = joined[:-STRIDE].reshape((patches, STRIDE) + tail_shape)
    upper = joined[STRIDE:].reshape((patches, STRIDE) + tail_shape)
    return jnp.concatenate([lower, upper], 1)


def per_device(
    byte_rows, cotangent, doc_ids, conv_weight, norm_gain, proj_weight, round_seed, step_count
):
    byte_block = byte_rows[0]
    upstream = cotangent[0]
    doc_block = doc_ids[0]
    length = byte_block.shape[0]
    row_width = byte_block.shape[1]
    patches = length // STRIDE
    panel_rows = proj_weight.shape[0]
    full_width = panel_rows * lax.axis_size("fsdp")
    next_bytes, next_up, next_docs = shifted(
        (byte_block[:STRIDE], upstream[:STRIDE], doc_block[:STRIDE]), "seq", -1
    )
    window = tap_windows(byte_block, next_bytes, patches)
    up_window = tap_windows(upstream, next_up, patches)
    doc_window = tap_windows(doc_block, next_docs, patches)
    is_last = lax.axis_index("seq") == lax.axis_size("seq") - 1
    patch_ids = lax.broadcasted_iota(jnp.int32, (patches, KERNEL), 0)
    tap_ids = lax.broadcasted_iota(jnp.int32, (patches, KERNEL), 1)
    spilled = is_last & (patch_ids == patches - 1) & (tap_ids >= STRIDE)
    keep_tap = (doc_window == doc_window[:, :1]) & jnp.logical_not(spilled)
    keep_f = keep_tap.astype(jnp.float32)[:, :, None]
    masked = window * keep_tap.astype(jnp.bfloat16)[:, :, None]
    grouped = masked.reshape(patches, KERNEL, GROUPS, CG)
    hidden = jnp.einsum(
        "pkgc,kgcd->pgd", grouped, conv_weight, preferred_element_type=jnp.float32
    ).reshape(patches, row_width)
    factor = lax.rsqrt(jnp.mean(hidden * hidden, axis=-1, keepdims=True) + 1e-06)
    normed = (hidden * factor * norm_gain).astype(jnp.bfloat16)
    contract_last = (((1,), (1,)), ((), ()))
    full_proj = lax.all_gather(proj_weight, "fsdp", axis=0, tiled=True)
    pre_act = lax.dot_general(normed, full_proj, contract_last, preferred_element_type=jnp.float32)
    grad_pre = (
        up_window.astype(jnp.float32)
        * keep_f
        * gelu_grad(pre_act.reshape(patches, KERNEL, row_width))
    )
    grad_pre = grad_pre.reshape(patches, full_width).astype(jnp.bfloat16)
    grad_norm = jnp.dot(grad_pre, full_proj, preferred_element_type=jnp.float32)
    contract_first = (((0,), (0,)), ((), ()))
    panel_part = lax.psum_scatter(
        lax.dot_general(grad_pre, normed, contract_first, preferred_element_type=jnp.float32),
        "fsdp",
        scatter_dimension=0,
        tiled=True,
    )
    proj_sum = lax.psum(panel_part, "seq")
    gain_part = jnp.sum(grad_norm * hidden * factor, axis=0)
    gained = norm_gain * grad_norm
    grad_hidden = factor * gained - hidden * factor * factor * factor * jnp.mean(
        gained * hidden, axis=-1, keepdims=True
    )
    grad_hidden = grad_hidden.reshape(patches, GROUPS, CG)
    grouped_f = grouped.astype(jnp.float32)
    conv_f = conv_weight.astype(jnp.float32)
    conv_part = jnp.einsum(
        "pkgc,pgd->kgcd", grouped_f, grad_hidden, precision=lax.Precision.HIGHEST
    )
    gain_sum, conv_sum = lax.psum((gain_part, conv_part), ("seq", "fsdp"))
    grad_window = jnp.einsum("pgd,kgcd->pkgc", grad_hidden, conv_f, precision=lax.Precision.HIGHEST)
    grad_window = grad_window.reshape(patches, KERNEL, row_width) * keep_f
    back_lower = grad_window[:, :STRIDE].reshape(length, row_width)
    back_upper = grad_window[:, STRIDE:].reshape(length, row_width)
    incoming = shifted(back_upper[length - STRIDE :], "seq", 1)
    back_rows = back_lower + jnp.concatenate([incoming, back_upper[: length - STRIDE]], 0)
    grad_bytes = (upstream.astype(jnp.float32) + back_rows)[None]
    total_patches = patches * lax.axis_size("seq") * lax.axis_size("fsdp")
    grad_scale = 1.0 / math.sqrt(total_patches)
    first_panel = lax.axis_index("fsdp") * jnp.int32(panel_rows)
    row_index = first_panel + jnp.arange(panel_rows, dtype=jnp.int32)
    flat_index = (
        row_index[:, None] * jnp.int32(row_width) + jnp.arange(row_width, dtype=jnp.int32)[None, :]
    )
    dither_noise = mix_bits(flat_index, round_seed[0], step_count[0])
    grad_proj = proj_sum * grad_scale + QUANT * (dither_noise - 0.5)
    return (grad_bytes, grad_proj, conv_sum * grad_scale, gain_sum * grad_scale)


def solution(mesh):
    in_specs = (
        P("fsdp", "seq", None),
        P("fsdp", "seq", None),
        P("fsdp", "seq"),
        P(),
        P(),
        P("fsdp", None),
        P(),
        P(),
    )
    out_specs = (P("fsdp", "seq", None), P("fsdp", None), P(), P())
    return jax.shard_map(
        per_device, mesh=mesh, in_specs=in_specs, out_specs=out_specs, check_vma=False
    )
```

profile of v0, /device:TPU:0, one launch (start us, length us, event | category | flops | bytes accessed | tf_op | source)
XLA Modules:
  0.0 380.3 jit_solution(10041539172174745510)
XLA Ops:
  7.2 0.7 all-gather.2.cloned.1.call-update
  7.9 0.7 slice_bitcast_fusion.2
  8.6 1.3 collective-permute-start.1
  9.9 0.7 slice_bitcast_fusion.1
  10.6 1.3 collective-permute-start
  11.9 0.7 slice_bitcast_fusion
  12.6 1.3 collective-permute-start.2
  13.9 9.7 %concatenate.46 = bf16[256,4,32,16]{3,2,1,0:T(8,128)(2,1)} reshape(bf16[1,1024,512]{2,1,0:T(8,128)(2,1)} %param.8) | data formatting | bytes 2097152 | tf_op jit(solution)/shard_map/concatenate | solution.py:51
  24.4 0.7 reduce.6
  25.3 9.9 %copy.43 = bf16[256,4,32,16]{0,3,2,1:T(8,128)(2,1)} copy(bf16[256,4,32,16]{3,2,1,0:T(8,128)(2,1)} %concatenate.46) | data formatting | bytes 2097152 | tf_op jit(solution)/shard_map/concatenate | solution.py:51
  35.2 3.1 copy.65
  38.4 1.2 copy.49
  40.4 8.2 %concatenate.48 = bf16[256,4,32,16]{3,2,1,0:T(8,128)(2,1)} reshape(bf16[1024,512]{1,0:T(8,128)(2,1)S(1)} %pad_maximum_fusion.1) | data formatting | bytes 2097152 | tf_op jit(solution)/shard_map/concatenate | solution.py:51
  48.6 9.8 %copy.44 = bf16[256,4,32,16]{0,3,2,1:T(8,128)(2,1)} copy(bf16[256,4,32,16]{3,2,1,0:T(8,128)(2,1)} %concatenate.48) | data formatting | bytes 2097152 | tf_op jit(solution)/shard_map/concatenate | solution.py:51
  58.9 1.2 copy.50
  61.0 1.0 copy-done.9
  62.1 0.8 fusion.21
  62.8 0.8 copy-done.4
  63.8 7.9 %fusion.6 = bf16[256,8,512]{2,0,1:T(8,128)(2,1)} fusion(bf16[256,512,1]{0,1,2:T(8,128)(2,1)S(1)} %bitcast.62, bf16[8,512,512]{2,1,0:T(8,128)(2,1)} %bitcast.67, bf16[256,4,512]{2,0,1:T(8,128)(2,1)} %copy.50, bf16[256,4,512]{2,0,1:T(8,128)(2,1)} %copy.49, f32[256,8]{0,1:T(8,128)S(1)} %get-tuple-element.18), kind=kOutput, calls=%fused_computation.8 | convolution fusion | flops 1096810496 | bytes 8658944 | tf_op jit(solution)/shard_map/dot_general | solution.py:86
  71.7 3.9 %copy.52 = bf16[256,8,512]{0,2,1:T(8,128)(2,1)} copy(bf16[256,8,512]{2,0,1:T(8,128)(2,1)} %fusion.6) | data formatting | bytes 4194304 | tf_op jit(solution)/shard_map/convert_element_type | solution.py:92
  75.6 6.1 %fusion.27 = f32[4096,512]{1,0:T(8,128)} fusion(bf16[256,4096]{0,1:T(8,128)(2,1)} %bitcast.55, bf16[256,512]{0,1:T(8,128)(2,1)S(1)} %bitcast.63), kind=kOutput, calls=%fused_computation.54 | convolution fusion | flops 1073741824 | bytes 10747904 | tf_op jit(solution)/shard_map/dot_general | solution.py:96
  82.0 3.5 copy.56
  86.8 2.0 copy.53
  88.8 4.3 %multiply_reduce_fusion = (f32[512]{0:T(512)S(1)}, f32[256]{0:T(256)S(1)}, f32[256,512]{1,0:T(8,128)S(1)}) fusion(f32[256,512]{1,0:T(8,128)} %copy.53, f32[256]{0:T(256)S(1)} %add_rsqrt_fusion, f32[512]{0:T(512)S(1)} %copy-done.13, bf16[256,4096]{0,1:T(8,128)(2,1)} %bitcast.56, bf16[4096,512]{1,0:T(8,128)(2,1)} %all-gather.2.cloned.1.call-done), kind=kOutput, calls=%fused_computation.36 | convolution fusion | flops 1074527488 | bytes 7346176 | tf_op jit(solution)/shard_map/dot_general | solution.py:93
  93.2 1.0 multiply_subtract_fusion
  94.2 2.2 copy.55
  96.4 9.8 %fusion.10 = f32[8,32,16,16]{2,3,0,1:T(8,128)} fusion(f32[256,32,16,1]{0,2,3,1:T(8,128)} %bitcast.59, bf16[256,8,32,16]{0,3,2,1:T(8,128)(2,1)S(1)} %maximum_multiply_fusion), kind=kOutput, calls=%fused_computation.16 | convolution fusion | flops 201326592 | bytes 2883584 | tf_op jit(solution)/shard_map/pkgc,pgd->kgcd/dot_general | solution.py:110
  106.2 1.0 copy-done.5
  107.5 1.8 convolution_bitcast_fusion
  109.3 2.6 copy.57
  111.9 5.4 %copy.58 = f32[256,8,512]{2,0,1:T(8,128)} copy(f32[256,8,512]{0,2,1:T(8,128)} %bitcast.54) | data formatting | bytes 8388608 | tf_op jit(solution)/shard_map/reshape | solution.py:115
  117.2 61.2 %reduce-scatter.2.cloned.1.call-done = f32[512,512]{1,0:T(8,128)} async-done(((f32[4096,512]{1,0:T(8,128)}), f32[512,512]{1,0:T(8,128)}) %reduce-scatter.2.cloned.1.call-update) | async-done | bytes 1048592 | tf_op jit(solution)/shard_map/reduce_scatter | solution.py:95
  178.5 2.5 broadcast_multiply_fusion
  181.0 1.9 copy-done
  183.0 3.4 collective-permute-start.3
  186.4 37.6 %psum.23 = f32[512]{0:T(512)S(1)} all-reduce(f32[512]{0:T(512)S(1)} %get-tuple-element.16), channel_id=1, replica_groups=mesh['seq'=4,'fsdp'=8] {'seq','fsdp'}, use_global_device_ids=true, to_apply=%region_6.0 | all-reduce | flops 512 | bytes 4096 | tf_op jit(solution)/shard_map/psum | solution.py:113
  224.6 2.2 copy-done.1
  227.0 1.4 slice-done
  228.4 2.7 copy.59
  231.1 3.0 reshape.243
  234.1 2.7 copy.60
  236.7 3.1 concatenate.56
  239.8 3.5 fusion.7
  243.3 72.9 %all-reduce.5.cloned.1.call-done = f32[8,32,16,16]{2,3,0,1:T(8,128)} async-done(((f32[8,32,16,16]{2,3,0,1:T(8,128)}), f32[8,32,16,16]{2,3,0,1:T(8,128)}) %all-reduce.5.cloned.1.call-update) | async-done | bytes 262160 | tf_op jit(solution)/shard_map/psum | solution.py:113
  316.2 1.8 broadcast_multiply_fusion.1
  318.0 2.3 copy.63
  320.3 50.6 %all-reduce.3.cloned.1.call-done = f32[512,512]{1,0:T(8,128)} async-done(((f32[512,512]{1,0:T(8,128)}), f32[512,512]{1,0:T(8,128)}) %all-reduce.3.cloned.1.call-update) | async-done | bytes 1048592 | tf_op jit(solution)/shard_map/psum | solution.py:101
  370.9 2.9 fusion.20
  (61 shorter events, 5.0 us)
Async XLA Ops:
  7.2 56.6 %all-gather.2.cloned.1.call-start = ((), (), s32[]{:S(2)}) async-start(), calls=%async_computation.1 | async-start | bytes 4718592 | tf_op jit(solution)/shard_map/all_gather | solution.py:85
  7.9 170.6 %reduce-scatter.2.cloned.1.call-start = ((), (), s32[]{:S(2)}) async-start(), calls=%async_computation.2 | async-start | bytes 9437184 | tf_op jit(solution)/shard_map/reduce_scatter | solution.py:95
  8.6 31.1 %collective-permute-start.1 = (s32[4]{0:T(128)S(1)}, s32[4]{0:T(128)S(1)}, u32[]{:S(2)}, u32[]{:S(2)}) collective-permute-start(s32[4]{0:T(128)S(1)} %slice_bitcast_fusion.2), channel_id=1, source_target_pairs={{8,0},{16,8},{24,16},{9,1},{17,9},{25,17},{10,2},{18,10},{26,18},{... | collective-permute-start | bytes 56 | tf_op jit(solution)/shard_map/ppermute | solution.py:22
  10.6 29.5 %collective-permute-start = (bf16[4,512]{1,0:T(4,128)(2,1)S(1)}, bf16[4,512]{1,0:T(4,128)(2,1)S(1)}, u32[]{:S(2)}, u32[]{:S(2)}) collective-permute-start(bf16[4,512]{1,0:T(4,128)(2,1)S(1)} %slice_bitcast_fusion.1), channel_id=1, source_target_pairs={{8,0},{16,8},{24,16},{9,1},{17,9},{25,17},{10,2},{18,10},{26,18},{... | collective-permute-start | bytes 12296 | tf_op jit(solution)/shard_map/ppermute | solution.py:22
  12.6 45.8 %collective-permute-start.2 = (bf16[4,512]{1,0:T(4,128)(2,1)S(1)}, bf16[4,512]{1,0:T(4,128)(2,1)S(1)}, u32[]{:S(2)}, u32[]{:S(2)}) collective-permute-start(bf16[4,512]{1,0:T(4,128)(2,1)S(1)} %slice_bitcast_fusion), channel_id=1, source_target_pairs={{8,0},{16,8},{24,16},{9,1},{17,9},{25,17},{10,2},{18,10},{26,18},{... | collective-permute-start | bytes 12296 | tf_op jit(solution)/shard_map/ppermute | solution.py:22
  13.9 9.7 %copy-start.2 = (bf16[1,1024,512]{2,1,0:T(8,128)(2,1)S(1)}, bf16[1,1024,512]{2,1,0:T(8,128)(2,1)}, u32[]{:S(2)}) copy-start(bf16[1,1024,512]{2,1,0:T(8,128)(2,1)} %param.9) | copy-start | bytes 3145732
  23.6 0.8 copy-start.12
  25.3 13.0 %copy-start.13 = (f32[512]{0:T(512)S(1)}, f32[512]{0:T(512)}, u32[]{:S(2)}) copy-start(f32[512]{0:T(512)} %param.12) | copy-start | bytes 6148
  35.2 4.9 %copy-start.6 = (bf16[1,1024,512]{2,1,0:T(8,128)(2,1)S(1)}, bf16[1,1024,512]{2,1,0:T(8,128)(2,1)}, u32[]{:S(2)}) copy-start(bf16[1,1024,512]{2,1,0:T(8,128)(2,1)} %param.8) | copy-start | bytes 3145732
  58.9 1.4 copy-start.7
  58.9 1.9 copy-start.8
  60.8 1.2 copy-start.9
  62.8 0.8 copy-start.4
  81.7 234.5 %all-reduce.5.cloned.1.call-start = ((), (), s32[]{:S(2)}) async-start(), calls=%async_computation.4 | async-start | bytes 4194304 | tf_op jit(solution)/shard_map/psum | solution.py:113
  88.8 4.4 %copy-start.11 = (f32[256,512]{1,0:T(8,128)S(1)}, f32[256,512]{1,0:T(8,128)}, u32[]{:S(2)}) copy-start(f32[256,512]{1,0:T(8,128)} %copy.53) | copy-start | bytes 1572868
  106.1 1.0 copy-start.5
  106.1 1.4 copy-start.10
  106.2 264.7 %all-reduce.3.cloned.1.call-start = ((), (), s32[]{:S(2)}) async-start(), calls=%async_computation.3 | async-start | bytes 2097152 | tf_op jit(solution)/shard_map/psum | solution.py:101
  181.0 1.9 copy-start
  183.0 56.8 %collective-permute-start.3 = (f32[4,512]{1,0:T(4,128)S(1)}, f32[4,512]{1,0:T(4,128)S(1)}, u32[]{:S(2)}, u32[]{:S(2)}) collective-permute-start(f32[4,512]{1,0:T(4,128)S(1)} %bitcast.65), channel_id=1, source_target_pairs={{0,8},{8,16},{16,24},{1,9},{9,17},{17,25},{2,10},{10,18},{18,26},{... | collective-permute-start | bytes 24584 | tf_op jit(solution)/shard_map/ppermute | solution.py:22
  224.6 2.2 copy-start.1
  226.8 1.6 slice-start
  236.7 3.1 copy-start.3
Sparse Core Ops, SparseCore 0:
  9.6 49.8 all-gather.1
  81.8 96.5 reduce-scatter.1
  183.8 132.3 all-reduce.4
  319.4 51.4 all-reduce.2
where the time goes:
time: 382 us; the launch traced here: 380 us
  waiting for transfers between devices  185 us (48%)
  local copies, waits for them, and re-layouts  89.7 us (23%)
  blocking collectives  37.6 us (10%)
  matrix products  30.7 us (8%)
  between operations  15.3 us (4%)
  other arithmetic  13.9 us (4%)
  starting transfers between devices  7.56 us (2%)
    psum x1, waiting for transfers between devices, per_device(): gain_sum, conv_sum = lax.psum((gain_part, conv_part), ('seq', 'fsdp'))  72.9 us
    reduce_scatter x1, waiting for transfers between devices, per_device(): lax.psum_scatter(lax.dot_general(grad_pre, normed, contract_first, prefer...  61.2 us
    psum x1, waiting for transfers between devices, per_device(): proj_sum = lax.psum(panel_part, 'seq')  50.6 us
    concatenate x6, local copies, waits for them, and re-layouts, tap_windows(): return jnp.concatenate([lower, upper], 1)  37.8 us
    psum x1, blocking collectives, per_device(): gain_sum, conv_sum = lax.psum((gain_part, conv_part), ('seq', 'fsdp'))  37.6 us
    unnamed x33, local copies, waits for them, and re-layouts  17.5 us
    dot_general x1, matrix products, per_device(): jnp.einsum('pkgc,pgd->kgcd', grouped_f, grad_hidden, precision=lax.Precis...  9.75 us
    dot_general x1, matrix products, per_device(): lax.dot_general(normed, full_proj, contract_last, preferred_element_type=...  7.92 us
  transfers between devices with their start and end apart: 8, of which 3 were waited for; matrix products, arithmetic and copies ran while one was open for 27% of the time, Pallas kernels for 0%

commit v1 on v0

v1 whole, which is shorter than its diff:
```python
import functools
import math

import jax
import jax.numpy as jnp
from jax import lax
from jax.experimental import pallas as pl
from jax.experimental.pallas import tpu as pltpu
from jax.sharding import PartitionSpec as P

GROUPS = 32
KERNEL = 8
STRIDE = 4
CG = 16
D = GROUPS * CG

GELU_A = 0.7978845608028654
GELU_B = 0.044715
QUANT = 0.25

MESH = pl.DeviceIdType.MESH
BF = jnp.bfloat16
F32 = jnp.float32


def gelu_grad(values):
    tangent = jnp.tanh(GELU_A * (values + GELU_B * values * values * values))
    return 0.5 * (1.0 + tangent) + 0.5 * values * (1.0 - tangent * tangent) * GELU_A * (
        1.0 + 3.0 * GELU_B * values * values
    )


def mix_bits(flat_index, seed_value, step_value):
    hashed = (
        flat_index * jnp.int32(-1640531535)
        + seed_value * jnp.int32(-2048144777)
        + step_value * jnp.int32(-1028477379)
    )
    hashed = hashed ^ lax.shift_right_logical(hashed, jnp.int32(16))
    hashed = hashed * jnp.int32(2146121005)
    hashed = hashed ^ lax.shift_right_logical(hashed, jnp.int32(15))
    hashed = hashed * jnp.int32(-2073254261)
    hashed = hashed ^ lax.shift_right_logical(hashed, jnp.int32(16))
    return lax.shift_right_logical(hashed, jnp.int32(8)).astype(F32) / 16777216.0


def dot(a, b, ca, cb):
    return lax.dot_general(a, b, (((ca,), (cb,)), ((), ())), preferred_element_type=F32)


def wide(mask):
    return jnp.concatenate([mask] * (D // 128), axis=1)


def kernel(
    n_s, n_z, scale,
    x_ref, ct_ref, doc_ref, cw_ref, gain_ref, pw_ref, seed_ref, step_ref,
    gb_ref, gpo_ref, co_ref,
    xf, cf, df, hx, hc, hd, win, up, kp, wd, w, gpo, gps, ps, rs1, sf, own, rs2, zs, fin, dith,
    gn, hid, fac, norm, gh, hsend, hrecv,
    pacc, cp, cpx, c1, c2, c3, c4, c5,
    sem_l, sem_h, s1, r1, s2, r2, s3, r3, sg, rg, sn, ss, rs, sz, rz, sf_s, sf_r, sc, rc,
):
    s = lax.axis_index("seq")
    f = lax.axis_index("fsdp")
    z = f // 2
    c = f % 2
    length = ct_ref.shape[0]
    patches = length // STRIDE
    pr = pw_ref.shape[0]
    q = pr // n_s
    parts = D // pr
    half_rows = (D // 2) // n_s

    def copy(src, dst, send, recv, dev):
        cpy = pltpu.make_async_remote_copy(
            src_ref=src, dst_ref=dst, send_sem=send, recv_sem=recv, device_id=dev, device_id_type=MESH
        )
        cpy.start()

    def drain(ref, sem):
        pltpu.make_async_copy(ref, ref, sem).wait()

    partner = (s, 2 * z + 1 - c)
    mypart = pl.ds(pl.multiple_of(c * patches, patches), patches)

    def zdev(i):
        zi = lax.rem(z + i, n_z)
        return zi, (s, 2 * zi + c)

    def sdev(i):
        si = lax.rem(s + i, n_s)
        return si, (si, f)

    own_panel = pltpu.make_async_copy(pw_ref, w.at[f], sem_l.at[0])
    own_panel.start()

    barrier = pltpu.get_barrier_semaphore()
    pl.semaphore_signal(barrier, inc=1, device_id=partner, device_id_type=MESH)
    for i in range(1, n_z):
        pl.semaphore_signal(barrier, inc=1, device_id=zdev(i)[1], device_id_type=MESH)
    for i in range(1, n_s):
        pl.semaphore_signal(barrier, inc=1, device_id=sdev(i)[1], device_id_type=MESH)
    pl.semaphore_wait(barrier, 1 + (n_z - 1) + (n_s - 1))

    for i in range(1, n_z):
        _, dev = zdev(n_z - i)
        copy(pw_ref.at[pl.ds(pl.multiple_of(s * q, q), q)],
             w.at[f, pl.ds(pl.multiple_of(s * q, q), q)], s1.at[i], r1.at[z], dev)
    copy(pw_ref, w.at[f], s3.at[z], r3.at[z], partner)

    @pl.when(s > 0)
    def _():
        dev = (s - 1, f)
        copy(x_ref.at[pl.ds(0, 16)], hx, sem_h.at[0], sem_h.at[1], dev)
        copy(ct_ref.at[pl.ds(0, 16)], hc, sem_h.at[2], sem_h.at[3], dev)
        copy(doc_ref.at[:, pl.ds(0, 128)], hd, sem_h.at[4], sem_h.at[5], dev)

    for lb in range(4):
        xf[lb, pl.ds(0, length)] = x_ref[:, lb * 128:(lb + 1) * 128].astype(F32)
        cf[lb, pl.ds(0, length)] = ct_ref[:, lb * 128:(lb + 1) * 128].astype(F32)
    df[pl.ds(0, length)] = jnp.transpose(
        jnp.broadcast_to(doc_ref[...].astype(F32), (128, length)), (1, 0)
    )

    spread = (
        lax.broadcasted_iota(jnp.int32, (CG, 256), 1) % CG
        == lax.broadcasted_iota(jnp.int32, (CG, 256), 0)
    ).astype(F32).astype(BF)
    diag = (
        lax.broadcasted_iota(jnp.int32, (256, 256), 0) // CG
        == lax.broadcasted_iota(jnp.int32, (256, 256), 1) // CG
    )

    def build(kb, carry):
        piece = cw_ref[pl.ds(pl.multiple_of(kb * 256, 256), 256), :]
        wd[kb] = jnp.where(diag, dot(piece, spread, 1, 0), 0.0).astype(BF)
        return carry

    lax.fori_loop(0, 2 * KERNEL, build, 0)

    @pl.when(s == n_s - 1)
    def _():
        xf[:, pl.ds(length, 8)] = jnp.zeros((4, 8, 128), F32)
        cf[:, pl.ds(length, 8)] = jnp.zeros((4, 8, 128), F32)
        df[pl.ds(length, 8)] = jnp.full((8, 128), -1.0, F32)

    @pl.when(s < n_s - 1)
    def _():
        drain(hx, sem_h.at[1])
        drain(hc, sem_h.at[3])
        drain(hd, sem_h.at[5])
        top = hx[...].astype(F32)
        topc = hc[...].astype(F32)
        for lb in range(4):
            xf[lb, pl.ds(length, 8)] = top[:8, lb * 128:(lb + 1) * 128]
            cf[lb, pl.ds(length, 8)] = topc[:8, lb * 128:(lb + 1) * 128]
        df[pl.ds(length, 8)] = jnp.transpose(
            jnp.broadcast_to(hd[...].astype(F32), (128, 128)), (1, 0)
        )[:8]

    @pl.when(s > 0)
    def _():
        drain(hx, sem_h.at[0])
        drain(hc, sem_h.at[2])
        drain(hd, sem_h.at[4])

    def taps(ref, k):
        return jnp.concatenate(
            [ref[lb, pl.ds(k, patches, stride=STRIDE), :] for lb in range(4)], axis=1
        )

    first_doc = df[pl.ds(0, patches, stride=STRIDE), :]
    for k in range(KERNEL):
        keep = (df[pl.ds(k, patches, stride=STRIDE), :] == first_doc).astype(F32)
        kp[k] = keep
        kw = wide(keep)
        win[k] = (taps(xf, k) * kw).astype(BF)
        upk = (taps(cf, k) * kw).astype(BF)
        for part in range(parts):
            up[k * parts + part] = upk[:, part * pr:(part + 1) * pr]

    def forward(i, carry):
        zi = lax.rem(z + i, n_z)
        fi = 2 * zi + c
        piece = w.at[fi, pl.ds(pl.multiple_of(s * q, q), q)]
        drain(piece, r1.at[zi])
        for j in range(1, n_s):
            _, dev = sdev(j)
            copy(piece, piece, s2.at[zi], r2.at[zi], dev)
        return carry

    lax.fori_loop(1, n_z, forward, 0)

    hid[...] = jnp.zeros_like(hid)

    def conv(k, carry):
        for b in range(2):
            hid[:, b * 256:(b + 1) * 256] += dot(win[k, :, b * 256:(b + 1) * 256], wd[2 * k + b], 1, 0)
        return carry

    lax.fori_loop(0, KERNEL, conv, 0)
    hidden = hid[...]
    factor = lax.rsqrt(jnp.mean(hidden * hidden, axis=-1, keepdims=True) + 1e-06)
    fac[...] = jnp.broadcast_to(factor, (patches, 128))
    norm[mypart] = (hidden * factor * gain_ref[...]).astype(BF)
    copy(norm.at[mypart], norm.at[mypart], sn.at[0], sn.at[1], partner)
    gn[...] = jnp.zeros_like(gn)
    own_panel.wait()

    def panel(fi, dst):
        pre = dot(norm[mypart], w[fi], 1, 1)
        g = (up[fi].astype(F32) * gelu_grad(pre)).astype(BF)
        dst[...] = g
        gn[...] += dot(g, w[fi], 1, 0)

    def sums(zi):
        drain(gps.at[0], rg.at[zi])
        total = dot(gpo[zi], norm[...], 0, 0)
        sf[...] = total
        ps[zi] = total.astype(BF)
        own[zi] = sf[pl.ds(pl.multiple_of(s * q, q), q), :]
        for j in range(1, n_s):
            sj, dev = sdev(j)
            copy(ps.at[zi, pl.ds(pl.multiple_of(sj * q, q), q)], rs1.at[zi, s], ss.at[zi], rs.at[zi], dev)

    def step(i, carry):
        zi = lax.rem(z + i, n_z)

        @pl.when(i > 0)
        def _():
            drain(w.at[0, pl.ds(0, (n_s - 1) * q)], r2.at[zi])
            copy(w.at[2 * zi + c], w.at[2 * zi + c], s3.at[zi], r3.at[zi], partner)

        panel(2 * zi + c, gpo.at[zi, mypart])
        drain(w.at[0], r3.at[zi])
        panel(2 * zi + 1 - c, gps.at[zi])
        copy(gps.at[zi], gpo.at[zi, mypart], sg.at[zi], rg.at[zi], partner)

        @pl.when(i == 0)
        def _():
            drain(gh, sn.at[1])

        @pl.when(i > 0)
        def _():
            sums(lax.rem(z + i - 1, n_z))

        return carry

    lax.fori_loop(0, n_z, step, 0)
    sums(lax.rem(z + n_z - 1, n_z))

    hidden = hid[...]
    factor = fac[:, :1]
    grad_norm = gn[...]
    gain_part = jnp.sum(grad_norm * hidden * factor, axis=0, keepdims=True)
    gained = gain_ref[...] * grad_norm
    gh[...] = (
        factor * gained
        - hidden * (factor * factor * factor) * jnp.mean(gained * hidden, axis=-1, keepdims=True)
    ).astype(BF)

    def upper(t):
        return wide(kp[STRIDE + t]) * jnp.concatenate(
            [dot(gh[:, b * 256:(b + 1) * 256], wd[2 * (STRIDE + t) + b], 1, 1) for b in range(2)], axis=1
        )

    cols = lax.broadcasted_iota(jnp.int32, (128, 128), 1) // CG
    small = lax.broadcasted_iota(jnp.int32, (128, 128), 0) // CG == cols
    pacc[...] = jnp.zeros_like(pacc)

    def conv_back(k, carry):
        for b in range(4):
            lanes = slice(b * 128, (b + 1) * 128)
            full = jnp.where(small, dot(jnp.transpose(win[k, :, lanes], (1, 0)), gh[:, lanes], 1, 0), 0.0)
            full = full + pltpu.roll(full, 64, 1)
            full = full + pltpu.roll(full, 32, 1)
            full = full + pltpu.roll(full, 16, 1)
            pacc[lanes, :] = jnp.where(cols == k, full, pacc[lanes, :])
        return carry

    [conv_back(k, 0) for k in range(KERNEL)]
    cp[...] = jnp.zeros_like(cp)
    cp[:, :, pl.ds(0, half_rows), :] = pacc[...].reshape(2, n_s, half_rows, 128)
    for b in range(4):
        cp[0, 0, pl.ds(half_rows + b, 1), :] = gain_part[:, b * 128:(b + 1) * 128]
    copy(cp.at[1 - c], cpx, sc.at[0], rc.at[0], partner)

    def reduce_seq(i, carry):
        zi = lax.rem(z + i, n_z)
        drain(rs1.at[0, pl.ds(0, n_s - 1)], rs.at[zi])
        total = own[zi]
        for j in range(1, n_s):
            total = total + rs1[zi, sdev(j)[0]].astype(F32)

        @pl.when(i > 0)
        def _():
            zs[i] = total.astype(BF)
            copy(zs.at[i], rs2.at[z], sz.at[i], rz.at[i], (s, 2 * zi + c))

        @pl.when(i == 0)
        def _():
            own[z] = total

        return carry

    lax.fori_loop(0, n_z - 1, reduce_seq, 0)

    drain(cpx, rc.at[0])
    c1[...] = cp[c] + cpx[...]
    for j in range(1, n_s):
        sj, dev = sdev(j)
        copy(c1.at[sj], c2.at[s], sc.at[1], rc.at[1], dev)

    row = lax.broadcasted_iota(jnp.int32, (patches, D), 0)
    for t in range(STRIDE):
        hi = upper(t)
        hsend[pl.ds(t, 1), :] = hi[patches - 1:, :]
        lo = wide(kp[t]) * jnp.concatenate(
            [dot(gh[:, b * 256:(b + 1) * 256], wd[2 * t + b], 1, 1) for b in range(2)], axis=1
        )
        value = taps(cf, t) + lo + jnp.where(row == 0, 0.0, pltpu.roll(hi, 1, 0))
        for lb in range(4):
            xf[lb, pl.ds(t, patches, stride=STRIDE), :] = value[:, lb * 128:(lb + 1) * 128]

    @pl.when(s < n_s - 1)
    def _():
        copy(hsend, hrecv, sem_h.at[6], sem_h.at[7], (s + 1, f))

    lax.fori_loop(n_z - 1, n_z, reduce_seq, 0)

    drain(c2.at[pl.ds(0, n_s - 1)], rc.at[1])
    total = c1[s]
    for j in range(1, n_s):
        total = total + c2[sdev(j)[0]]
    c3[z] = total
    for i in range(1, n_z):
        copy(c3.at[z], c3.at[z], sc.at[2], rc.at[2], zdev(i)[1])

    for lb in range(4):
        gb_ref[:, lb * 128:(lb + 1) * 128] = xf[lb, pl.ds(0, length)]

    shape = (pr, D)
    flat = (f * pr + lax.broadcasted_iota(jnp.int32, shape, 0)) * jnp.int32(D) + lax.broadcasted_iota(
        jnp.int32, shape, 1
    )
    dith[...] = QUANT * (mix_bits(flat, seed_ref[0], step_ref[0]) - 0.5)

    drain(c3.at[pl.ds(0, n_z - 1)], rc.at[2])
    total = c3[0]
    for i in range(1, n_z):
        total = total + c3[i]
    c4[s] = total
    for j in range(1, n_s):
        copy(c4.at[s], c4.at[s], sc.at[3], rc.at[3], sdev(j)[1])

    total = own[z]
    for i in range(1, n_z):
        drain(rs2.at[0], rz.at[i])
        total = total + rs2[zdev(n_z - i)[0]].astype(F32)
    mine = pl.ds(pl.multiple_of(s * q, q), q)
    fin[mine] = total.astype(BF)
    for j in range(1, n_s):
        copy(fin.at[mine], fin.at[mine], sf_s.at[0], sf_r.at[0], sdev(j)[1])

    drain(c4.at[pl.ds(0, n_s - 1)], rc.at[3])
    copy(c4, c5, sc.at[4], rc.at[4], partner)

    @pl.when(s > 0)
    def _():
        drain(hrecv, sem_h.at[7])
        gb_ref[pl.ds(0, 8), :] += jnp.where(
            lax.broadcasted_iota(jnp.int32, (8, D), 0) < STRIDE, hrecv[...], 0.0
        )

    @pl.when(s < n_s - 1)
    def _():
        drain(hsend, sem_h.at[6])

    co_ref[c] = c4[...] * scale
    drain(c5, rc.at[4])
    co_ref[1 - c] = c5[...] * scale

    drain(fin.at[pl.ds(0, (n_s - 1) * q)], sf_r.at[0])
    gpo_ref[...] = fin[...].astype(F32) * scale + dith[...]

    for i in range(1, n_z):
        drain(w.at[0, pl.ds(0, q)], s1.at[i])
        drain(zs.at[0], sz.at[i])
        zi, _ = zdev(i)
        drain(w.at[0, pl.ds(0, (n_s - 1) * q)], s2.at[zi])
    for i in range(n_z):
        drain(w.at[0], s3.at[i])
        drain(gps.at[0], sg.at[i])
        drain(rs1.at[0, pl.ds(0, n_s - 1)], ss.at[i])
    drain(gh, sn.at[0])
    drain(cpx, sc.at[0])
    drain(c2.at[pl.ds(0, n_s - 1)], sc.at[1])
    drain(c3.at[pl.ds(0, n_z - 1)], sc.at[2])
    drain(c4.at[pl.ds(0, n_s - 1)], sc.at[3])
    drain(c4, sc.at[4])
    drain(fin.at[pl.ds(0, (n_s - 1) * q)], sf_s.at[0])


def per_device(
    n_s, n_f, byte_rows, cotangent, doc_ids, conv_weight, norm_gain, proj_weight, round_seed, step_count
):
    length = byte_rows.shape[1]
    patches = length // STRIDE
    pr = proj_weight.shape[0]
    n_z = n_f // 2
    q = pr // n_s
    rows = (D // 2) // n_s + 8
    scale = 1.0 / math.sqrt(patches * n_s * n_f)
    v = pltpu.VMEM
    dma = pltpu.SemaphoreType.DMA
    vm = pl.BlockSpec(memory_space=pltpu.VMEM)
    smem = pl.BlockSpec(memory_space=pltpu.SMEM)
    scratch = [
        v((4, length + 8, 128), F32), v((4, length + 8, 128), F32), v((length + 8, 128), F32),
        v((16, D), BF), v((16, D), BF), v((1, 128), jnp.int32),
        v((KERNEL, patches, D), BF), v((n_f, patches, pr), BF), v((KERNEL, patches, 128), F32),
        v((2 * KERNEL, 256, 256), BF), v((n_f, pr, D), BF),
        v((n_z, 2 * patches, pr), BF), v((n_z, patches, pr), BF),
        v((n_z, pr, D), BF), v((n_z, n_s, q, D), BF), v((pr, D), F32), v((n_z, q, D), F32),
        v((n_z, q, D), BF), v((n_z, q, D), BF), v((pr, D), BF), v((pr, D), F32),
        v((patches, D), F32), v((patches, D), F32), v((patches, 128), F32),
        v((2 * patches, D), BF), v((patches, D), BF),
        v((8, D), F32), v((8, D), F32),
        v((D, 128), F32), v((2, n_s, rows, 128), F32), v((n_s, rows, 128), F32),
        v((n_s, rows, 128), F32), v((n_s, rows, 128), F32), v((n_z, rows, 128), F32),
        v((n_s, rows, 128), F32), v((n_s, rows, 128), F32),
        dma((1,)), dma((8,)), dma((n_z,)), dma((n_z,)), dma((n_z,)), dma((n_z,)), dma((n_z,)), dma((n_z,)),
        dma((n_z,)), dma((n_z,)), dma((2,)), dma((n_z,)), dma((n_z,)), dma((n_z,)), dma((n_z,)),
        dma((1,)), dma((1,)), dma((5,)), dma((5,)),
    ]
    grad_bytes, grad_proj, packed = pl.pallas_call(
        functools.partial(kernel, n_s, n_z, scale),
        out_shape=(
            jax.ShapeDtypeStruct((length, D), F32),
            jax.ShapeDtypeStruct((pr, D), F32),
            jax.ShapeDtypeStruct((2, n_s, rows, 128), F32),
        ),
        in_specs=[vm, vm, vm, vm, vm, pl.BlockSpec(memory_space=pl.ANY), smem, smem],
        out_specs=(vm, vm, vm),
        scratch_shapes=scratch,
        compiler_params=pltpu.CompilerParams(
            collective_id=0, has_side_effects=True, vmem_limit_bytes=58 * 1024 * 1024
        ),
    )(
        byte_rows[0], cotangent[0], doc_ids, conv_weight.reshape(KERNEL * D, CG), norm_gain[None],
        proj_weight, round_seed, step_count,
    )
    grad_gain = packed[0, 0, rows - 8 : rows - 4].reshape(D)
    grad_conv = packed[:, :, : rows - 8].reshape(GROUPS, CG, KERNEL, CG).transpose(2, 0, 1, 3)
    return grad_bytes[None], grad_proj, grad_conv, grad_gain


def solution(mesh):
    in_specs = (
        P("fsdp", "seq", None),
        P("fsdp", "seq", None),
        P("fsdp", "seq"),
        P(),
        P(),
        P("fsdp", None),
        P(),
        P(),
    )
    out_specs = (P("fsdp", "seq", None), P("fsdp", None), P(), P())
    return jax.shard_map(
        functools.partial(per_device, mesh.shape["seq"], mesh.shape["fsdp"]),
        mesh=mesh, in_specs=in_specs, out_specs=out_specs, check_vma=False,
    )
```

time: 382 us -> 84.5 us (0.22)
  waiting for transfers between devices: 185 us -> 0 us
  local copies, waits for them, and re-layouts: 89.7 us -> 11.8 us
  Pallas kernels: 0 us -> 70.2 us
  blocking collectives: 37.6 us -> 0 us
  matrix products: 30.7 us -> 0 us
  other arithmetic: 13.9 us -> 0 us
  between operations: 15.3 us -> 1.95 us
  starting transfers between devices: 7.56 us -> 0 us
    psum x2 -> x0, waiting for transfers between devices: 123 us -> none  [the longest x1 72.9 us: per_device(): gain_sum, conv_sum = lax.psum((gain_part, conv_part), ('seq', 'fsdp'))]
    pallas_call x0 -> x1, Pallas kernels: none -> 70.2 us  [per_device(): pl.pallas_call(functools.partial(kernel, n_s, n_z, scale), out_shape=(jax...]
    reduce_scatter x1 -> x0, waiting for transfers between devices: 61.2 us -> none  [per_device(): lax.psum_scatter(lax.dot_general(grad_pre, normed, contract_first, prefer...]
    concatenate x7 -> x0, local copies, waits for them, and re-layouts: 40.9 us -> none  [the longest x6 37.8 us: tap_windows(): return jnp.concatenate([lower, upper], 1)]
    psum x1 -> x0, blocking collectives: 37.6 us -> none  [per_device(): gain_sum, conv_sum = lax.psum((gain_part, conv_part), ('seq', 'fsdp'))]
    dot_general x6 -> x0, matrix products: 30.7 us -> none  [the longest x1 9.75 us: per_device(): jnp.einsum('pkgc,pgd->kgcd', grouped_f, grad_hidden, precision=lax.Precis...]
    reshape x5 -> x1, local copies, waits for them, and re-layouts: 11.8 us -> 0.59 us  [per_device(): packed[:, :, :rows - 8].reshape(GROUPS, CG, KERNEL, CG)]
    unnamed x33 -> x6, local copies, waits for them, and re-layouts: 17.5 us -> 9.02 us
  transfers between devices with their start and end apart: 8 -> 0, of which waited for: 3 -> 0; matrix products, arithmetic and copies ran while one was open for 27% -> 0% of each run, Pallas kernels for 0% -> 0%
where the time goes in v1:
time: 84.5 us; the launch traced here: 84 us
  Pallas kernels  70.2 us (83%)
  local copies, waits for them, and re-layouts  11.8 us (14%)
  between operations  1.95 us (2%)
    pallas_call x1, Pallas kernels, per_device(): pl.pallas_call(functools.partial(kernel, n_s, n_z, scale), out_shape=(jax...  70.2 us
    unnamed x6, local copies, waits for them, and re-layouts  9.02 us

profile of v1, /device:TPU:0, one launch (start us, length us, event | category | flops | bytes accessed | tf_op | source)
XLA Modules:
  0.0 84.0 jit_solution(3068786740087201197)
XLA Ops:
  1.9 2.7 %copy.14 = bf16[8,32,16,16]{3,2,1,0:T(8,128)(2,1)} copy(bf16[8,32,16,16]{1,3,2,0:T(8,128)(2,1)} %param.11) | data formatting | bytes 262144 | tf_op args[3]
  4.7 70.2 %shard_map.111 = (f32[1024,512]{1,0:T(8,128)}, f32[512,512]{1,0:T(8,128)}, f32[2,4,72,128]{3,2,1,0:T(8,128)}) custom-call(bf16[1024,512]{1,0:T(8,128)(2,1)} %bitcast.13, bf16[1024,512]{1,0:T(8,128)(2,1)} %bitcast.14, s32[1,1024]{1,0:T(1,128)} %doc_ref.1, bf16[4096,16]{1,0:T(8,128)(2,1)} %bitcast.11, f32[1,512]{1,0:T(1,128)} %bitcast.15, ...), custom_call_target="tpu_custom_call" | custom-call | tf_op jit(solution)/shard_map/pallas_call | solution.py:437
  74.9 1.3 %slice_bitcast_fusion = f32[512]{0:T(512)} fusion(f32[2,4,72,128]{3,2,1,0:T(8,128)} %get-tuple-element.9), kind=kLoop, calls=%fused_computation | loop fusion | bytes 4096 | tf_op jit(solution)/shard_map/reshape;squeeze | solution.py:454
  76.1 1.0 %slice.6 = f32[2,4,64,128]{3,2,1,0:T(8,128)S(1)} slice(f32[2,4,72,128]{3,2,1,0:T(8,128)} %get-tuple-element.9), slice={[0:2], [0:4], [0:64], [0:128]} | slice | bytes 524288 | tf_op jit(solution)/shard_map/slice | solution.py:455
  77.1 0.6 reshape.15
  77.7 2.1 %copy.15 = f32[8,32,16,16]{1,3,2,0:T(8,128)} copy(f32[8,32,16,16]{3,0,2,1:T(8,128)S(1)} %bitcast.10) | data formatting | bytes 524288
  79.8 0.0 copy-start
  79.8 3.2 %copy.20 = f32[1,1024,512]{2,1,0:T(8,128)} copy(f32[1,1024,512]{2,1,0:T(8,128)} %bitcast.12) | data formatting | bytes 4194304
  83.0 0.0 copy-done
  83.0 1.0 %copy.21 = f32[512,512]{1,0:T(8,128)} copy(f32[512,512]{1,0:T(8,128)S(1)} %copy-done) | data formatting | bytes 2097152
Async XLA Ops:
  79.8 3.2 %copy-start = (f32[512,512]{1,0:T(8,128)S(1)}, f32[512,512]{1,0:T(8,128)}, u32[]{:S(2)}) copy-start(f32[512,512]{1,0:T(8,128)} %get-tuple-element.19) | copy-start | bytes 3145732
